TPU v7x, 256 devices: a whole 4x4x8 slice. The times are simulated.
256 devices in a mesh: expert: 16 (over y, x), tensor: 8 (over z), dp: 2 (over core).
Axes of the slice: x: 4, y: 4, z: 8, core: 2. Of those that a mesh axis runs over, the one named last changes fastest.
Arguments:
- moe_input: bfloat16 [2048, 3072], P('expert', ('tensor', 'dp')), may hold values from -6 to 6
- grad_out: bfloat16 [2048, 3072], P('expert', ('tensor', 'dp')), may hold values from -6 to 6
- expert_ids: int32 [2048, 4], P('expert'), may hold values from 0 to 15, all different within a row; in each aligned block of 128 rows (0 to 127, 128 to 255, ...) at most 64 rows name the same one
- route_weight: float32 [2048, 4], P('expert'), may hold values from 0.1 to 1
- gate_pre: bfloat16 [2048, 4, 6144], P('expert', None, ('tensor', 'dp')), may hold values from -8 to 8
- up_weight: bfloat16 [16, 3072, 6144], P('expert', None, ('tensor', 'dp')), may hold values from -0.109375 to 0.109375
- down_weight: bfloat16 [16, 3072, 6144], P('expert', None, ('tensor', 'dp')), may hold values from -0.078125 to 0.078125
Outputs:
- input_grad: bfloat16 [2048, 3072], P('expert', ('tensor', 'dp'))
- gate_grad: bfloat16 [2048, 4, 6144], P('expert', None, ('tensor', 'dp'))
- up_grad: bfloat16 [16, 3072, 6144], P('expert', None, ('tensor', 'dp'))
- down_grad: bfloat16 [16, 3072, 6144], P('expert', None, ('tensor', 'dp'))
Inputs may be any that keep to these rules, and one draw needn't show every extreme that they name: `expert_ids`: each row names 4 different experts. Among the 128 rows of one device (aligned blocks of 128 rows) no expert is named by more than 64 rows, and in every draw some expert is named by exactly 64 rows of some device.
All inputs are finite; a program needn't handle non-finite values.
Results may differ from a plain program's by a relative error of at most 0.02.
Values may be sent and summed in bfloat16 or wider, within the bound.
A program may use at most 128 MiB of HBM per device.

v0:
```python
import jax
import jax.numpy as jnp
from jax import lax
from jax.sharding import PartitionSpec as P


def silu_terms(gate_value):
    sigmoid = jax.nn.sigmoid(gate_value)
    return (gate_value * sigmoid, sigmoid * (1.0 + gate_value * (1.0 - sigmoid)))


def local(moe_input, grad_out, expert_ids, route_weight, gate_pre, up_weight, down_weight):
    expert_count = lax.axis_size("expert")
    token_count, route_width = expert_ids.shape
    capacity = min(token_count, 2 * token_count * route_width // expert_count)
    route_count = token_count * route_width
    flat_ids = expert_ids.reshape(route_count)
    one_hot = (flat_ids[:, None] == jnp.arange(expert_count, dtype=jnp.int32)[None, :]).astype(
        jnp.int32
    )
    earlier = jnp.cumsum(one_hot, axis=0) - one_hot
    slot_index = flat_ids * capacity + jnp.sum(earlier * one_hot, axis=1)
    token_of = jnp.arange(route_count, dtype=jnp.int32) // route_width
    flat_weight = route_weight.reshape(route_count, 1)
    gate_rows = gate_pre.reshape(route_count, gate_pre.shape[2])

    def to_slots(values):
        return (
            jnp.zeros((expert_count * capacity, values.shape[1]), values.dtype)
            .at[slot_index]
            .set(values)
        )

    input_rows = moe_input[token_of]
    delta_rows = (flat_weight * grad_out[token_of].astype(jnp.float32)).astype(jnp.bfloat16)
    received = (
        lax.all_to_all(to_slots(input_rows), "expert", split_axis=0, concat_axis=0, tiled=True),
        lax.all_to_all(to_slots(delta_rows), "expert", split_axis=0, concat_axis=0, tiled=True),
        lax.all_to_all(to_slots(gate_rows), "expert", split_axis=0, concat_axis=0, tiled=True),
    )
    inputs_full, deltas_full = (
        lax.all_gather(received[0], ("tensor", "dp"), axis=1, tiled=True),
        lax.all_gather(received[1], ("tensor", "dp"), axis=1, tiled=True),
    )
    gate_got = received[2]
    w_up = up_weight[0]
    w_down = down_weight[0]
    up = jnp.dot(inputs_full, w_up, preferred_element_type=jnp.float32)
    act, slope = silu_terms(gate_got.astype(jnp.float32))
    hidden = (act * up).astype(jnp.bfloat16)
    dhid = jnp.dot(deltas_full, w_down, preferred_element_type=jnp.float32)
    up_delta = (dhid * act).astype(jnp.bfloat16)
    gate_delta = (dhid * up * slope).astype(jnp.bfloat16)
    partial_value = lax.dot_general(
        up_delta, w_up, (((1,), (1,)), ((), ())), preferred_element_type=jnp.float32
    )
    up_grad = lax.dot_general(
        inputs_full, up_delta, (((0,), (0,)), ((), ())), preferred_element_type=jnp.float32
    ).astype(jnp.bfloat16)
    down_grad = lax.dot_general(
        deltas_full, hidden, (((0,), (0,)), ((), ())), preferred_element_type=jnp.float32
    ).astype(jnp.bfloat16)
    summed = lax.psum_scatter(
        partial_value.astype(jnp.bfloat16), ("tensor", "dp"), scatter_dimension=1, tiled=True
    ).astype(jnp.float32)
    returned = lax.all_to_all(
        summed.astype(jnp.bfloat16), "expert", split_axis=0, concat_axis=0, tiled=True
    ).astype(summed.dtype)
    token_total = jnp.sum(returned[slot_index].reshape(token_count, route_width, -1), axis=1)
    gate_returned = lax.all_to_all(gate_delta, "expert", split_axis=0, concat_axis=0, tiled=True)
    input_grad = (grad_out.astype(jnp.float32) + token_total).astype(jnp.bfloat16)
    gate_grad = gate_returned[slot_index].reshape(token_count, route_width, -1)
    return (input_grad, gate_grad, up_grad[None], down_grad[None])


def solution(mesh):
    in_specs = (
        P("expert", ("tensor", "dp")),
        P("expert", ("tensor", "dp")),
        P("expert", None),
        P("expert", None),
        P("expert", None, ("tensor", "dp")),
        P("expert", None, ("tensor", "dp")),
        P("expert", None, ("tensor", "dp")),
    )
    out_specs = (
        P("expert", ("tensor", "dp")),
        P("expert", None, ("tensor", "dp")),
        P("expert", None, ("tensor", "dp")),
        P("expert", None, ("tensor", "dp")),
    )
    return jax.shard_map(local, mesh=mesh, in_specs=in_specs, out_specs=out_specs, check_vma=False)
```

profile of v0, /device:TPU:1, one launch (start us, length us, event | category | flops | bytes accessed | tf_op | source)
XLA Modules:
  0.0 236.8 jit_solution(9547321273398463361)
XLA Ops:
  7.2 0.0 copy-start
  7.2 0.0 all-gather.5.cloned.1.call-start
  7.2 0.9 copy.34
  8.2 0.1 eq.29
  8.3 0.1 eq.25
  8.4 0.7 broadcast_multiply_fusion
  9.1 1.2 reduce-window.6
  10.3 0.2 slice_reduce_fusion
  10.5 0.1 copy.33
  10.6 0.1 mul.52
  10.8 0.9 copy.41
  11.7 0.1 fusion.24
  11.8 3.9 %scatter_custom_fusion.2 = bf16[1024,192]{1,0:T(8,128)(2,1)S(1)} fusion(s32[512]{0:T(512)S(1)} %bitcast.66, bf16[128,192]{1,0:T(8,128)(2,1)S(1)} %copy.41, s32[1024]{0:T(1024)S(1)} %pad_clamp_fusion.1, bf16[]{:T(256)} %constant.26.clone.1), kind=kCustom, calls=%fused_computation.34 | custom fusion | bytes 393218 | tf_op jit(solution)/shard_map/scatter | solution.py:31
  15.7 17.9 %all_to_all.54 = bf16[16,64,192]{2,1,0:T(8,128)(2,1)S(1)} all-to-all(bf16[16,64,192]{2,1,0:T(8,128)(2,1)S(1)} %bitcast.64), channel_id=1, replica_groups=mesh['expert'=16,'tensor'=8,'dp'=2] {'expert'}, dimensions={0} | all-to-all | bytes 786432 | tf_op jit(solution)/shard_map/all_to_all | solution.py:37
  33.6 0.9 copy.42
  34.5 0.0 all-gather.5.cloned.1.call-update
  34.6 0.0 all-gather.3.cloned.1.call-start
  34.6 0.1 copy.32
  34.8 0.1 copy.37
  34.9 0.1 mul.54
  35.0 4.0 %scatter_custom_fusion = bf16[1024,192]{1,0:T(8,128)(2,1)S(1)} fusion(s32[512]{0:T(512)S(1)} %bitcast.67, f32[512]{0:T(512)S(1)} %mul.54, bf16[]{:T(256)} %constant.26.clone.1, bf16[128,192]{1,0:T(8,128)(2,1)S(1)} %copy.32, s32[1024]{0:T(1024)S(1)} %pad_clamp_fusion.1), kind=kCustom, calls=%fused_computation.33 | custom fusion | flops 294912 | bytes 464898 | tf_op jit(solution)/shard_map/scatter | solution.py:31
  39.0 13.1 %all_to_all.55 = bf16[16,64,192]{2,1,0:T(8,128)(2,1)S(1)} all-to-all(bf16[16,64,192]{2,1,0:T(8,128)(2,1)S(1)} %bitcast.63), channel_id=1, replica_groups=mesh['expert'=16,'tensor'=8,'dp'=2] {'expert'}, dimensions={0} | all-to-all | bytes 786432 | tf_op jit(solution)/shard_map/all_to_all | solution.py:38
  52.1 1.0 copy.39
  53.1 0.0 all-gather.3.cloned.1.call-update
  53.1 1.1 reshape.172
  54.2 3.3 %scatter_custom_fusion.1 = bf16[1024,384]{1,0:T(8,128)(2,1)} fusion(s32[512]{0:T(512)S(1)} %bitcast.68, bf16[512,384]{1,0:T(8,128)(2,1)S(1)} %reshape.172, bf16[]{:T(256)} %constant.26.clone.1), kind=kCustom, calls=%fused_computation.31 | custom fusion | bytes 786434 | tf_op jit(solution)/shard_map/scatter | solution.py:31
  57.5 3.6 %all-to-all-start.1 = ((bf16[16,64,384]{2,1,0:T(8,128)(2,1)}), bf16[16,64,384]{2,1,0:T(8,128)(2,1)S(1)}, u32[]{:S(2)}, u32[]{:S(2)}) async-start(bf16[16,64,384]{2,1,0:T(8,128)(2,1)} %bitcast.7), calls=%async_computation.1 | async-start | bytes 1572864 | tf_op jit(solution)/shard_map/all_to_all | solution.py:39
  61.1 0.2 reduce-scatter.2.cloned.1.call-start
  61.3 20.2 %all-gather.5.cloned.1.call-done = bf16[1024,3072]{0,1:T(8,128)(2,1)} async-done(((bf16[1024,192]{0,1:T(8,128)(2,1)}), bf16[1024,3072]{0,1:T(8,128)(2,1)}) %all-gather.5.cloned.1.call-update) | async-done | bytes 6291472 | tf_op jit(solution)/shard_map/all_gather | solution.py:42
  81.6 6.7 %fusion.2 = f32[1024,384]{1,0:T(8,128)} fusion(bf16[1024,3072]{0,1:T(8,128)(2,1)} %all-gather.5.cloned.1.call-done, bf16[1,3072,384]{2,1,0:T(8,128)(2,1)S(1)} %copy-done), kind=kOutput, calls=%fused_computation.15 | convolution fusion | flops 2415919104 | bytes 10223616 | tf_op jit(solution)/shard_map/dot_general | solution.py:48
  88.3 39.8 %all-gather.3.cloned.1.call-done = bf16[1024,3072]{0,1:T(8,128)(2,1)} async-done(((bf16[1024,192]{0,1:T(8,128)(2,1)}), bf16[1024,3072]{0,1:T(8,128)(2,1)}) %all-gather.3.cloned.1.call-update) | async-done | bytes 6291472 | tf_op jit(solution)/shard_map/all_gather | solution.py:43
  128.1 9.2 %fusion.13 = (bf16[1024,384]{1,0:T(8,128)(2,1)}, bf16[1024,384]{1,0:T(8,128)(2,1)S(1)}, f32[1024,384]{1,0:T(8,128)}) fusion(f32[1024,384]{1,0:T(8,128)} %fusion.2, bf16[16,64,384]{2,1,0:T(8,128)(2,1)S(1)} %all-to-all-done.1, bf16[1024,3072]{0,1:T(8,128)(2,1)} %all-gather.3.cloned.1.call-done, bf16[1,3072,384]{2,1,0:T(8,128)(2,1)} %param.13), kind=kOutput, calls=%fused_computation.26 | convolution fusion | flops 2421424128 | bytes 14155776 | tf_op jit(solution)/shard_map/dot_general | solution.py:51
  137.3 0.9 copy-done.5
  138.2 5.3 %convolution_convert_fusion = bf16[1024,3072]{0,1:T(8,128)(2,1)} fusion(bf16[1024,384]{1,0:T(8,128)(2,1)S(1)} %get-tuple-element.13, bf16[1,3072,384]{2,1,0:T(8,128)(2,1)S(1)} %copy-done), kind=kOutput, calls=%fused_computation.7 | convolution fusion | flops 2419064832 | bytes 9437184 | tf_op jit(solution)/shard_map/dot_general | solution.py:54
  143.5 0.0 reduce-scatter.2.cloned.1.call-update
  143.6 6.5 %all-to-all-start.4 = ((bf16[16,64,384]{2,1,0:T(8,128)(2,1)}), bf16[16,64,384]{2,1,0:T(8,128)(2,1)S(1)}, u32[]{:S(2)}, u32[]{:S(2)}) async-start(bf16[16,64,384]{2,1,0:T(8,128)(2,1)} %bitcast.65), calls=%async_computation.5 | async-start | bytes 1572864 | tf_op jit(solution)/shard_map/all_to_all | solution.py:70
  150.1 8.7 %fusion.1 = bf16[1,3072,384]{2,1,0:T(8,128)(2,1)} fusion(bf16[1024,3072]{0,1:T(8,128)(2,1)} %all-gather.3.cloned.1.call-done, f32[1024,384]{1,0:T(8,128)} %get-tuple-element.14, f32[1024,384]{1,0:T(8,128)} %fusion.2), kind=kOutput, calls=%fused_computation.11 | convolution fusion | flops 2417885184 | bytes 11796480 | tf_op jit(solution)/shard_map/dot_general | solution.py:60
  158.9 46.9 %reduce-scatter.2.cloned.1.call-done = bf16[1024,192]{0,1:T(8,128)(2,1)} async-done(((bf16[1024,3072]{0,1:T(8,128)(2,1)}), bf16[1024,192]{0,1:T(8,128)(2,1)}) %reduce-scatter.2.cloned.1.call-update) | async-done | bytes 393232 | tf_op jit(solution)/shard_map/reduce_scatter | solution.py:63
  205.7 2.0 copy.40
  207.7 6.4 %all-to-all-start.2 = ((bf16[16,64,192]{2,1,0:T(8,128)(2,1)}), bf16[16,64,192]{2,1,0:T(8,128)(2,1)}, u32[]{:S(2)}, u32[]{:S(2)}) async-start(bf16[16,64,192]{2,1,0:T(8,128)(2,1)} %bitcast.60), calls=%async_computation.3 | async-start | bytes 1048576 | tf_op jit(solution)/shard_map/all_to_all | solution.py:66
  214.1 7.8 %fusion = bf16[1,3072,384]{2,1,0:T(8,128)(2,1)} fusion(bf16[1024,3072]{0,1:T(8,128)(2,1)} %all-gather.5.cloned.1.call-done, bf16[1024,384]{1,0:T(8,128)(2,1)} %copy-done.5), kind=kOutput, calls=%fused_computation.10 | convolution fusion | flops 2417098752 | bytes 9437184 | tf_op jit(solution)/shard_map/dot_general | solution.py:57
  221.9 1.9 gather_fusion.1
  223.8 0.8 reshape.125
  224.7 1.1 bitcast_convert_fusion
  225.8 2.2 gather_fusion
  228.0 1.2 reshape.124
  229.2 0.3 reduce_sum.22
  229.6 0.7 copy.43
  (21 shorter events, 0.1 us)
Async XLA Ops:
  7.2 74.4 %copy-start = (bf16[1,3072,384]{2,1,0:T(8,128)(2,1)S(1)}, bf16[1,3072,384]{2,1,0:T(8,128)(2,1)}, u32[]{:S(2)}) copy-start(bf16[1,3072,384]{2,1,0:T(8,128)(2,1)} %param.12) | copy-start | bytes 7077892
  7.2 27.4 %copy-start.3 = (bf16[128,192]{0,1:T(8,128)(2,1)S(1)}, bf16[128,192]{0,1:T(8,128)(2,1)}, u32[]{:S(2)}) copy-start(bf16[128,192]{0,1:T(8,128)(2,1)} %param.8) | copy-start | bytes 147460
  7.2 27.5 %copy-start.4 = (f32[128,4]{0,1:T(4,128)S(1)}, f32[128,4]{0,1:T(4,128)}, u32[]{:S(2)}) copy-start(f32[128,4]{0,1:T(4,128)} %param.10) | copy-start | bytes 6148
  7.2 74.4 %all-gather.5.cloned.1.call-start = ((), (), s32[]{:S(2)}) async-start(), calls=%async_computation.8 | async-start | bytes 6684672 | tf_op jit(solution)/shard_map/all_gather | solution.py:42
  34.6 93.5 %all-gather.3.cloned.1.call-start = ((), (), s32[]{:S(2)}) async-start(), calls=%async_computation.6 | async-start | bytes 6684672 | tf_op jit(solution)/shard_map/all_gather | solution.py:43
  34.7 4.3 %copy-start.1 = (bf16[128,192]{1,0:T(8,128)(2,1)}, bf16[128,192]{1,0:T(8,128)(2,1)S(1)}, u32[]{:S(2)}) copy-start(bf16[128,192]{1,0:T(8,128)(2,1)S(1)} %copy.32) | copy-start | bytes 147460
  57.5 30.8 %all-to-all-start.1 = ((bf16[16,64,384]{2,1,0:T(8,128)(2,1)}), bf16[16,64,384]{2,1,0:T(8,128)(2,1)S(1)}, u32[]{:S(2)}, u32[]{:S(2)}) async-start(bf16[16,64,384]{2,1,0:T(8,128)(2,1)} %bitcast.7), calls=%async_computation.1 | async-start | bytes 1572864 | tf_op jit(solution)/shard_map/all_to_all | solution.py:39
  61.1 144.6 %reduce-scatter.2.cloned.1.call-start = ((), (), s32[]{:S(2)}) async-start(), calls=%async_computation.7 | async-start | bytes 6684672 | tf_op jit(solution)/shard_map/reduce_scatter | solution.py:63
  137.3 0.9 copy-start.5
  143.6 64.2 %all-to-all-start.4 = ((bf16[16,64,384]{2,1,0:T(8,128)(2,1)}), bf16[16,64,384]{2,1,0:T(8,128)(2,1)S(1)}, u32[]{:S(2)}, u32[]{:S(2)}) async-start(bf16[16,64,384]{2,1,0:T(8,128)(2,1)} %bitcast.65), calls=%async_computation.5 | async-start | bytes 1572864 | tf_op jit(solution)/shard_map/all_to_all | solution.py:70
  207.7 16.9 %all-to-all-start.2 = ((bf16[16,64,192]{2,1,0:T(8,128)(2,1)}), bf16[16,64,192]{2,1,0:T(8,128)(2,1)}, u32[]{:S(2)}, u32[]{:S(2)}) async-start(bf16[16,64,192]{2,1,0:T(8,128)(2,1)} %bitcast.60), calls=%async_computation.3 | async-start | bytes 1048576 | tf_op jit(solution)/shard_map/all_to_all | solution.py:66
  225.8 3.8 %copy-start.2 = (bf16[128,192]{1,0:T(8,128)(2,1)S(1)}, bf16[128,192]{1,0:T(8,128)(2,1)}, u32[]{:S(2)}) copy-start(bf16[128,192]{1,0:T(8,128)(2,1)} %copy-done.1) | copy-start | bytes 147460
Sparse Core Ops, SparseCore 0:
  34.7 46.8 all-gather.4
  83.4 44.6 all-gather.2
  143.7 61.9 reduce-scatter.1
where the time goes:
time: 240 us; the launch traced here: 237 us
  waiting for transfers between devices  107 us (45%)
  matrix products  37.8 us (16%)
  blocking collectives  31 us (13%)
  local copies, waits for them, and re-layouts  22.9 us (10%)
  starting transfers between devices  16.8 us (7%)
  between operations  14 us (6%)
  other arithmetic  7.46 us (3%)
    reduce_scatter x1, waiting for transfers between devices, local(): lax.psum_scatter(partial_value.astype(jnp.bfloat16), ('tensor', 'dp'), sc...  46.9 us
    all_gather x1, waiting for transfers between devices, local(): lax.all_gather(received[1], ('tensor', 'dp'), axis=1, tiled=True)  39.8 us
    all_gather x1, waiting for transfers between devices, local(): lax.all_gather(received[0], ('tensor', 'dp'), axis=1, tiled=True)  20.2 us
    all_to_all x1, blocking collectives, local(): lax.all_to_all(to_slots(input_rows), 'expert', split_axis=0, concat_axis=...  17.9 us
    all_to_all x1, blocking collectives, local(): lax.all_to_all(to_slots(delta_rows), 'expert', split_axis=0, concat_axis=...  13.1 us
    dot_general x1, matrix products, local(): dhid = jnp.dot(deltas_full, w_down, preferred_element_type=jnp.float32)  9.22 us
    dot_general x1, matrix products, local(): lax.dot_general(deltas_full, hidden, (((0,), (0,)), ((), ())), preferred_...  8.74 us
    dot_general x1, matrix products, local(): lax.dot_general(inputs_full, up_delta, (((0,), (0,)), ((), ())), preferre...  7.79 us
  transfers between devices with their start and end apart: 6, of which 3 were waited for; matrix products, arithmetic and copies ran while one was open for 16% of the time, Pallas kernels for 0%

commit v1 on v0

v1 whole, which is shorter than its diff:
```python
import functools

import jax
import jax.numpy as jnp
from jax import lax
from jax.experimental import pallas as pl
from jax.experimental.pallas import tpu as pltpu
from jax.sharding import PartitionSpec as P

MESH = pl.DeviceIdType.MESH
F32 = jnp.float32
BF16 = jnp.bfloat16
NE = 16
CAP = 64
TOK = 128
ROWS = NE * CAP
CH = 384
GROUP = 256
GROUPS = ROWS // GROUP
PER = GROUP // CAP
NT = (((1,), (1,)), ((), ()))
TN = (((0,), (0,)), ((), ()))


def xor(a, b):
    total = 0
    for bit in (1, 2, 4, 8):
        total = total + bit * lax.rem(lax.div(a, bit) + lax.div(b, bit), 2)
    return total


def block(k):
    return pl.ds(pl.multiple_of(k * CAP, CAP), CAP)


def group_rows(g):
    return pl.ds(pl.multiple_of(g * GROUP, GROUP), GROUP)


def kernel(
    x_ref, g_ref, ids_ref, w_ref, gate_ref, wu_hbm, wd_hbm,
    ig_ref, gg_ref, ug_hbm, dg_hbm,
    wu, wd, s_tok, s_route, w_slot, swap_out, swap_in, t4, slots, xd,
    gate_out, gate_in, gd_out, gd_in, up_s, hid, upd, ps, qd, zs, zr, xs, tr, tk, fr, grads,
    w_sem, swap_sem, a1_s, a1_r, gate_s, gate_r, xy_s, xy_r, za_s, za_r, zb_s, zb_r,
    own_s, own_r, opp_s, opp_r, rd_s, rd_r, rza_s, rza_r, rzb_s, rzb_r, rx_s, rx_r,
    rg_s, rg_r, fin_s, fin_r, out_sem,
):
    me = lax.axis_index("expert")
    z = lax.axis_index("tensor")
    c = lax.axis_index("dp")
    p = lax.rem(z, 2)
    mz = lax.div(z, 2)
    sib = 1 - c
    right = lax.rem(z + 1, 8)
    left = lax.rem(z + 7, 8)

    def copy(src, dst, send, recv, **ids):
        return pltpu.make_async_remote_copy(
            src_ref=src, dst_ref=dst, send_sem=send, recv_sem=recv, device_id=ids, device_id_type=MESH
        )

    bar = pltpu.get_barrier_semaphore()

    def greet(**ids):
        pl.semaphore_signal(bar, inc=1, device_id=ids, device_id_type=MESH)

    greet(dp=sib)
    for j in range(1, 4):
        greet(tensor=lax.rem(z + 2 * j, 8))
        greet(tensor=lax.rem(z + 2 * j, 8), dp=sib)
    greet(tensor=right)
    greet(tensor=left)

    @pl.loop(1, NE)
    def _(k):
        greet(expert=xor(me, k))

    def weight_copies():
        made = []
        for i, (src, dst) in enumerate(((wu_hbm, wu), (wd_hbm, wd))):
            for q in range(8):
                made.append(
                    pltpu.make_async_copy(
                        src.at[0, pl.ds(q * CH, CH)],
                        dst.at[q % 2, pl.ds((q // 2) * CH, CH)],
                        w_sem.at[i * 8 + q],
                    )
                )
        return made

    for made in weight_copies():
        made.start()

    lane = lax.broadcasted_iota(jnp.int32, (TOK, TOK), 1)
    sub = lax.broadcasted_iota(jnp.int32, (TOK, TOK), 0)
    ids = ids_ref[...].astype(F32)
    wts = w_ref[...]
    ids_pad = jnp.zeros((TOK, TOK), F32)
    w_pad = jnp.zeros((TOK, TOK), F32)
    for j in range(4):
        ids_pad = jnp.where(lane == j, ids[:, j : j + 1], ids_pad)
        w_pad = jnp.where(lane == j, wts[:, j : j + 1], w_pad)
    ids_t = ids_pad.T[0:8]
    w_t = w_pad.T[0:8]
    earlier = (sub < lane).astype(BF16)
    hits = []
    experts = [xor(me, k).astype(F32) for k in range(NE)]
    for k in range(NE):
        hits.append([(ids_t[j : j + 1] == experts[k]).astype(F32) for j in range(4)])
    named = jnp.concatenate([h[0] + h[1] + h[2] + h[3] for h in hits], axis=0)
    rank = jnp.dot(named.astype(BF16), earlier, preferred_element_type=F32)
    place = lax.broadcasted_iota(jnp.int32, (CAP, TOK), 0).astype(F32)
    for k in range(NE):
        here = jnp.where((rank[k : k + 1] == place) & (named[k : k + 1] > 0.5), 1.0, 0.0)
        rows = slice(k * CAP, (k + 1) * CAP)
        s_tok[rows] = here.astype(BF16)
        weight = jnp.zeros((1, TOK), F32)
        for j in range(4):
            s_route[rows, j * TOK : (j + 1) * TOK] = (here * hits[k][j]).astype(BF16)
            weight = weight + hits[k][j] * w_t[j : j + 1]
        col = jnp.sum(here * weight, axis=1, keepdims=True)
        w_slot[rows] = jnp.where(c == 0, jnp.ones((CAP, TOK), F32), jnp.broadcast_to(col, (CAP, TOK)))

    pl.semaphore_wait(bar, 24)

    xv = x_ref[...].astype(F32)
    gv = g_ref[...].astype(F32)
    is0 = c == 0
    own_half = jnp.where(is0, xv, gv)
    swap_out[...] = jnp.where(is0, gv, xv).astype(BF16)
    swap = copy(swap_out, swap_in, swap_sem.at[0], swap_sem.at[1], dp=sib)
    swap.start()

    def gate_copy(k):
        return copy(gate_out.at[block(k)], gate_in.at[block(k)], gate_s.at[k], gate_r.at[k], expert=xor(me, k))

    swap.wait_recv()
    got = swap_in[...].astype(F32)
    t4[mz] = jnp.concatenate(
        [jnp.where(is0, own_half, got), jnp.where(is0, got, own_half)], axis=1
    ).astype(BF16)

    def a1_copy(j):
        return copy(t4.at[mz], t4.at[mz], a1_s.at[j - 1], a1_r.at[j - 1], tensor=lax.rem(z + 2 * j, 8))

    for j in (2, 1, 3):
        a1_copy(j).start()

    @pl.loop(0, GROUPS)
    def _(g):
        value = jnp.dot(s_route[group_rows(g)], gate_ref[...], preferred_element_type=F32)
        gate_out[group_rows(g)] = value.astype(BF16)

        @pl.when(g == 0)
        def _():
            gate_in[0:CAP] = value[0:CAP].astype(BF16)

        for i in range(PER):
            k = g * PER + i

            @pl.when(k > 0)
            def _():
                gate_copy(k).start()

    def a1_arrival(j):
        src = lax.rem(mz + 4 - j, 4)
        return copy(t4.at[src], t4.at[src], a1_s.at[j - 1], a1_r.at[j - 1], tensor=lax.rem(z + 2 * j, 8))

    for j in (1, 3, 2):
        a1_arrival(j).wait_recv()

    def xy_copy(k):
        return copy(slots.at[block(k)], xd.at[c, p, block(k)], xy_s.at[k], xy_r.at[k], expert=xor(me, k))

    @pl.loop(0, GROUPS)
    def _(g):
        rows = group_rows(g)
        for m in range(4):
            value = jnp.dot(s_tok[rows], t4[m], preferred_element_type=F32)
            scale = w_slot[rows]
            value = (value * jnp.concatenate([scale] * (CH // TOK), axis=1)).astype(BF16)
            slots[rows, m * CH : (m + 1) * CH] = value

            @pl.when(g == 0)
            def _():
                xd[c, p, 0:CAP, m * CH : (m + 1) * CH] = value[0:CAP]

        for i in range(PER):
            k = g * PER + i

            @pl.when(k > 0)
            def _():
                xy_copy(k).start()

    def za_copy(k, par):
        at = xd.at[c, par, block(k), pl.ds(0, 768)]
        return copy(at, at, za_s.at[k], za_r.at[k], tensor=right)

    def zb_copy(k, par):
        at = xd.at[c, par, block(k), pl.ds(768, 768)]
        return copy(at, at, zb_s.at[k], zb_r.at[k], tensor=left)

    def own_copy(k, arr):
        at = xd.at[arr, p, block(k)]
        return copy(at, at, own_s.at[k], own_r.at[k], dp=sib)

    def opp_copy(k, arr):
        at = xd.at[arr, 1 - p, block(k)]
        return copy(at, at, opp_s.at[k], opp_r.at[k], dp=sib)

    def rd_copy(g):
        return copy(ps.at[sib, g], qd.at[g], rd_s.at[g], rd_r.at[g], dp=sib)

    def rza_copy(g):
        return copy(zs.at[g, 0], zr.at[g, 0], rza_s.at[g], rza_r.at[g], tensor=right)

    def rzb_copy(g):
        return copy(zs.at[g, 1], zr.at[g, 1], rzb_s.at[g], rzb_r.at[g], tensor=left)

    def rx_copy(k):
        return copy(xs.at[:, block(k)], tr.at[:, block(k)], rx_s.at[k], rx_r.at[k], expert=xor(me, k))

    def rg_copy(k):
        return copy(gd_out.at[block(k)], gd_in.at[block(k)], rg_s.at[k], rg_r.at[k], expert=xor(me, k))

    def compute_up(g):
        rows = group_rows(g)

        @pl.when(g == 0)
        def _():
            for made in weight_copies():
                made.wait()

        up_s[...] = jnp.dot(xd[0, 0, rows], wu[0], preferred_element_type=F32) + jnp.dot(
            xd[0, 1, rows], wu[1], preferred_element_type=F32
        )

    def compute_down(g):
        rows = group_rows(g)
        for i in range(PER):
            k = g * PER + i

            @pl.when(k > 0)
            def _():
                gate_copy(k).wait_recv()

        dhid = jnp.dot(xd[1, 0, rows], wd[0], preferred_element_type=F32) + jnp.dot(
            xd[1, 1, rows], wd[1], preferred_element_type=F32
        )
        up = up_s[...]
        gate = gate_in[rows].astype(F32)
        s = 1.0 / (1.0 + jnp.exp(-gate))
        act = gate * s
        hid[rows] = (act * up).astype(BF16)
        upd[rows] = (dhid * act).astype(BF16)
        delta = (dhid * up * (s * (1.0 + gate * (1.0 - s)))).astype(BF16)
        gd_out[rows] = delta

        @pl.when(g == 0)
        def _():
            gd_in[0:CAP] = delta[0:CAP]

        for i in range(PER):
            k = g * PER + i

            @pl.when(k > 0)
            def _():
                rg_copy(k).start()

    def compute_partial(g):
        value = upd[group_rows(g)]
        for m in range(4):
            for par in range(2):
                ps[m % 2, g, par, m // 2] = lax.dot_general(
                    value, wu[par, m * CH : (m + 1) * CH], NT, preferred_element_type=F32
                ).astype(BF16)
        rd_copy(g).start()

    def return_z(g):
        rd_copy(g).wait_recv()
        for mm in range(2):
            total = ps[c, g, 1 - p, mm].astype(F32) + qd[g, 1 - p, mm].astype(F32)
            zs[g, mm] = total.astype(BF16)
        rza_copy(g).start()
        rzb_copy(g).start()

    def return_xy(g):
        rza_copy(g).wait_recv()
        rzb_copy(g).wait_recv()
        rows = group_rows(g)
        for mm in range(2):
            total = ps[c, g, p, mm].astype(F32) + qd[g, p, mm].astype(F32) + zr[g, mm].astype(F32)
            value = total.astype(BF16)
            xs[mm, rows] = value

            @pl.when(g == 0)
            def _():
                tr[mm, 0:CAP] = value[0:CAP]

        for i in range(PER):
            k = g * PER + i

            @pl.when(k > 0)
            def _():
                rx_copy(k).start()

    def grad(a, par, m):
        left_side = xd[a, par, :, m * CH : (m + 1) * CH]
        right_side = (upd if a == 0 else hid)[...]
        q = 2 * m + par
        rows = slice(q * CH, (q + 1) * CH)
        grads[a, rows] = lax.dot_general(left_side, right_side, TN, preferred_element_type=F32).astype(BF16)
        grad_copy(a, q).start()

    def grad_copy(a, q):
        rows = pl.ds(q * CH, CH)
        return pltpu.make_async_copy(grads.at[a, rows], (ug_hbm, dg_hbm)[a].at[0, rows], out_sem.at[a * 8 + q])

    jobs = [(a, par, m) for a in range(2) for m in range(4) for par in range(2)]
    LAG_Z, LAG_S, LAG_C = 2, 3, 4
    FIRST = PER - 1 + LAG_C

    @pl.loop(0, FIRST + 4 * (GROUPS - 1) + 3)
    def _(step):
        @pl.when(step < NE)
        def _():
            @pl.when(step > 0)
            def _():
                xy_copy(step).wait_recv()

            za_copy(step, p).start()
            zb_copy(step, p).start()
            own_copy(step, c).start()

        @pl.when((step >= LAG_Z) & (step < NE + LAG_Z))
        def _():
            k = step - LAG_Z
            za_copy(k, 1 - p).wait_recv()
            zb_copy(k, 1 - p).wait_recv()
            opp_copy(k, c).start()

        @pl.when((step >= LAG_S) & (step < NE + LAG_S))
        def _():
            k = step - LAG_S
            own_copy(k, sib).wait_recv()
            opp_copy(k, sib).wait_recv()

        @pl.when(step >= FIRST)
        def _():
            turn = step - FIRST
            g = lax.div(turn, 4)
            phase = lax.rem(turn, 4)

            @pl.when(phase == 0)
            def _():
                compute_up(g)

                @pl.when(g > 0)
                def _():
                    return_xy(g - 1)

            @pl.when(phase == 1)
            def _():
                compute_down(g)

            @pl.when(phase == 2)
            def _():
                compute_partial(g)

            @pl.when(phase == 3)
            def _():
                return_z(g)

    last = GROUPS - 1
    for job in jobs[0:3]:
        grad(*job)
    return_z(last)
    for job in jobs[3:7]:
        grad(*job)
    return_xy(last)
    for job in jobs[7:12]:
        grad(*job)

    @pl.loop(1, NE)
    def _(k):
        rx_copy(k).wait_recv()

    def fin_dest(mm):
        return 2 * (c + 2 * mm) + p

    def fin_copy(mm, h):
        return copy(
            tk.at[mm, h], fr.at[mz], fin_s.at[mm * 2 + h], fin_r.at[mz], tensor=fin_dest(mm), dp=jnp.int32(h)
        )

    def fin_local(mm, h):
        return (fin_dest(mm) == z) & (c == h)

    for mm in range(2):
        total = lax.dot_general(s_tok[...], tr[mm], TN, preferred_element_type=F32)
        for h in range(2):
            value = total[:, h * 192 : (h + 1) * 192].astype(BF16)
            tk[mm, h] = value

            @pl.when(fin_local(mm, h))
            def _():
                fr[mz] = value

            @pl.when(jnp.logical_not(fin_local(mm, h)))
            def _():
                fin_copy(mm, h).start()

    for job in jobs[12:16]:
        grad(*job)

    @pl.loop(1, NE)
    def _(k):
        rg_copy(k).wait_recv()

    gg_ref[...] = lax.dot_general(s_route[...], gd_in[...], TN, preferred_element_type=F32).astype(BF16)

    swap.wait_send()
    for j in range(1, 4):
        a1_copy(j).wait_send()

    @pl.loop(0, NE)
    def _(k):
        za_copy(k, p).wait_send()
        zb_copy(k, p).wait_send()
        own_copy(k, c).wait_send()
        opp_copy(k, c).wait_send()

        @pl.when(k > 0)
        def _():
            gate_copy(k).wait_send()
            xy_copy(k).wait_send()
            rx_copy(k).wait_send()
            rg_copy(k).wait_send()

    @pl.loop(0, GROUPS)
    def _(g):
        rd_copy(g).wait_send()
        rza_copy(g).wait_send()
        rzb_copy(g).wait_send()

    for a in range(2):
        for q in range(8):
            grad_copy(a, q).wait()

    for src in range(4):
        @pl.when(jnp.logical_not((mz == src) & (c == lax.rem(mz, 2))))
        def _():
            copy(
                fr.at[src], fr.at[src], fin_s.at[0], fin_r.at[src], tensor=right
            ).wait_recv()

    total = g_ref[...].astype(F32)
    for src in range(4):
        total = total + fr[src].astype(F32)
    ig_ref[...] = total.astype(BF16)

    for mm in range(2):
        for h in range(2):
            @pl.when(jnp.logical_not(fin_local(mm, h)))
            def _():
                fin_copy(mm, h).wait_send()


def local(moe_input, grad_out, expert_ids, route_weight, gate_pre, up_weight, down_weight):
    gates = jnp.swapaxes(gate_pre, 0, 1).reshape(4 * TOK, CH)
    vmem = pl.BlockSpec(memory_space=pltpu.VMEM)
    anywhere = pl.BlockSpec(memory_space=pl.ANY)
    dma = pltpu.SemaphoreType.DMA

    def scratch(*shape, dtype=BF16):
        return pltpu.VMEM(shape, dtype)

    input_grad, gate_rows, up_grad, down_grad = pl.pallas_call(
        kernel,
        out_shape=(
            jax.ShapeDtypeStruct((TOK, 192), BF16),
            jax.ShapeDtypeStruct((4 * TOK, CH), BF16),
            jax.ShapeDtypeStruct(up_weight.shape, BF16),
            jax.ShapeDtypeStruct(down_weight.shape, BF16),
        ),
        in_specs=[vmem] * 5 + [anywhere] * 2,
        out_specs=(vmem, vmem, anywhere, anywhere),
        scratch_shapes=[
            scratch(2, 4 * CH, CH),
            scratch(2, 4 * CH, CH),
            scratch(ROWS, TOK),
            scratch(ROWS, 4 * TOK),
            scratch(ROWS, TOK, dtype=F32),
            scratch(TOK, 192),
            scratch(TOK, 192),
            scratch(4, TOK, CH),
            scratch(ROWS, 4 * CH),
            scratch(2, 2, ROWS, 4 * CH),
            scratch(ROWS, CH),
            scratch(ROWS, CH),
            scratch(ROWS, CH),
            scratch(ROWS, CH),
            scratch(GROUP, CH, dtype=F32),
            scratch(ROWS, CH),
            scratch(ROWS, CH),
            scratch(2, GROUPS, 2, 2, GROUP, CH),
            scratch(GROUPS, 2, 2, GROUP, CH),
            scratch(GROUPS, 2, GROUP, CH),
            scratch(GROUPS, 2, GROUP, CH),
            scratch(2, ROWS, CH),
            scratch(2, ROWS, CH),
            scratch(2, 2, TOK, 192),
            scratch(4, TOK, 192),
            scratch(2, 8 * CH, CH),
            dma((16,)),
            dma((2,)),
            dma((3,)), dma((3,)),
            dma((NE,)), dma((NE,)),
            dma((NE,)), dma((NE,)),
            dma((NE,)), dma((NE,)),
            dma((NE,)), dma((NE,)),
            dma((NE,)), dma((NE,)),
            dma((NE,)), dma((NE,)),
            dma((GROUPS,)), dma((GROUPS,)),
            dma((GROUPS,)), dma((GROUPS,)),
            dma((GROUPS,)), dma((GROUPS,)),
            dma((NE,)), dma((NE,)),
            dma((NE,)), dma((NE,)),
            dma((4,)), dma((4,)),
            dma((16,)),
        ],
        compiler_params=pltpu.CompilerParams(
            collective_id=0, has_side_effects=True, vmem_limit_bytes=60 * 1024 * 1024
        ),
        name="routed_backward",
    )(moe_input, grad_out, expert_ids, route_weight, gates, up_weight, down_weight)
    gate_grad = jnp.swapaxes(gate_rows.reshape(4, TOK, CH), 0, 1)
    return input_grad, gate_grad, up_grad, down_grad


def solution(mesh):
    sharded = P("expert", ("tensor", "dp"))
    cube = P("expert", None, ("tensor", "dp"))
    rows = P("expert", None)
    return jax.shard_map(
        local,
        mesh=mesh,
        in_specs=(sharded, sharded, rows, rows, cube, cube, cube),
        out_specs=(sharded, cube, cube, cube),
        check_vma=False,
    )
```

time: 240 us -> 161 us (0.67); the launches traced: 237 us -> 160 us
  Pallas kernels: 0 us -> 144 us
  waiting for transfers between devices: 107 us -> 0 us
  matrix products: 37.8 us -> 0 us
  blocking collectives: 31 us -> 0 us
  starting transfers between devices: 16.8 us -> 0 us
  between operations: 14 us -> 0.64 us
  other arithmetic: 7.46 us -> 0 us
  local copies, waits for them, and re-layouts: 22.9 us -> 16.1 us
    pallas_call x0 -> x1, Pallas kernels: none -> 144 us  [local(): pl.pallas_call(kernel, out_shape=(jax.ShapeDtypeStruct((TOK, 192), BF16),...]
    all_gather x2 -> x0, waiting for transfers between devices: 60 us -> none  [the longest x1 39.8 us: local(): lax.all_gather(received[1], ('tensor', 'dp'), axis=1, tiled=True)]
    reduce_scatter x1 -> x0, waiting for transfers between devices: 46.9 us -> none  [local(): lax.psum_scatter(partial_value.astype(jnp.bfloat16), ('tensor', 'dp'), sc...]
    dot_general x5 -> x0, matrix products: 37.8 us -> none  [the longest x1 9.22 us: local(): dhid = jnp.dot(deltas_full, w_down, preferred_element_type=jnp.float32)]
    all_to_all x2 -> x0, blocking collectives: 31 us -> none  [the longest x1 17.9 us: local(): lax.all_to_all(to_slots(input_rows), 'expert', split_axis=0, concat_axis=...]
    all_to_all x3 -> x0, starting transfers between devices: 16.5 us -> none  [the longest x1 6.54 us: local(): lax.all_to_all(gate_delta, 'expert', split_axis=0, concat_axis=0, tiled=T...]
    unnamed x17 -> x9, local copies, waits for them, and re-layouts: 3.69 us -> 12.3 us
    scatter x2 -> x0, local copies, waits for them, and re-layouts: 7.22 us -> none  [to_slots(): return jnp.zeros((expert_count * capacity, values.shape[1]), values.dtype...]
  transfers between devices with their start and end apart: 6 -> 0, of which waited for: 3 -> 0; matrix products, arithmetic and copies ran while one was open for 16% -> 0% of each run, Pallas kernels for 0% -> 0%
where the time goes in v1:
time: 161 us; the launch traced here: 160 us
  Pallas kernels  144 us (89%)
  local copies, waits for them, and re-layouts  16.1 us (10%)
    pallas_call x1, Pallas kernels, local(): pl.pallas_call(kernel, out_shape=(jax.ShapeDtypeStruct((TOK, 192), BF16),...  144 us
    unnamed x9, local copies, waits for them, and re-layouts  12.3 us

profile of v1, /device:TPU:1, one launch (start us, length us, event | category | flops | bytes accessed | tf_op | source)
XLA Modules:
  0.0 160.5 jit_solution(14607517488608838180)
XLA Ops:
  0.6 1.5 copy.12.x_ref
  2.2 1.5 copy.13.g_ref
  3.7 1.4 copy.14.ids_ref
  5.1 1.4 copy.15.w_ref
  6.5 1.8 %copy.11 = bf16[4,128,384]{2,1,0:T(8,128)(2,1)} copy(bf16[4,128,384]{2,0,1:T(4,128)(2,1)} %bitcast.7) | data formatting | bytes 786432 | tf_op jit(solution)/shard_map/transpose | solution.py:471
  8.3 143.7 %routed_backward.1 = (bf16[128,192]{1,0:T(8,128)(2,1)}, bf16[512,384]{1,0:T(8,128)(2,1)}, bf16[1,3072,384]{2,1,0:T(8,128)(2,1)}, bf16[1,3072,384]{2,1,0:T(8,128)(2,1)}) custom-call(bf16[128,192]{1,0:T(8,128)(2,1)} %copy.12.x_ref, bf16[128,192]{1,0:T(8,128)(2,1)} %copy.13.g_ref, s32[128,4]{1,0:T(8,128)} %copy.14.ids_ref, f32[128,4]{1,0:T(8,128)} %copy.15.w_ref, ...), custom_call_target="tpu_custom_call" | custom-call | tf_op jit(solution)/shard_map/routed_backward/pallas_call | solution.py:479
  152.0 1.6 copy.17
  153.6 2.0 %copy.19 = bf16[4,128,384]{2,0,1:T(4,128)(2,1)} copy(bf16[4,128,384]{2,1,0:T(8,128)(2,1)} %bitcast.9) | data formatting | bytes 786432 | tf_op jit(solution)/shard_map/reshape | solution.py:538
  155.6 0.0 copy-start
  155.6 3.5 %copy.22 = bf16[1,3072,384]{2,1,0:T(8,128)(2,1)} copy(bf16[1,3072,384]{2,1,0:T(8,128)(2,1)} %get-tuple-element.22) | data formatting | bytes 4718592
  159.1 0.0 copy-done
  159.1 1.4 copy.23
Async XLA Ops:
  155.6 3.5 %copy-start = (bf16[1,3072,384]{2,1,0:T(8,128)(2,1)S(1)}, bf16[1,3072,384]{2,1,0:T(8,128)(2,1)}, u32[]{:S(2)}) copy-start(bf16[1,3072,384]{2,1,0:T(8,128)(2,1)} %get-tuple-element.23) | copy-start | bytes 7077892

commit v2 on v1

--- a/solution.py
+++ b/solution.py
@@ -16,16 +16,19 @@
 ROWS = NE * CAP
 CH = 384
 GROUP = 256
+WINDOW = 8
 GROUPS = ROWS // GROUP
 PER = GROUP // CAP
 NT = (((1,), (1,)), ((), ()))
 TN = (((0,), (0,)), ((), ()))
 
 
-def xor(a, b):
+def partner(me, k):
+    k0, k1, k2, k3 = (lax.rem(lax.div(k, bit), 2) for bit in (1, 2, 4, 8))
+    flips = (k0 + k1 + k2, k1 + k3, k0 + k1, k1)
     total = 0
-    for bit in (1, 2, 4, 8):
-        total = total + bit * lax.rem(lax.div(a, bit) + lax.div(b, bit), 2)
+    for i, flip in enumerate(flips):
+        total = total + 2**i * lax.rem(lax.div(me, 2**i) + flip, 2)
     return total
 
 
@@ -38,11 +41,12 @@
 
 
 def kernel(
-    x_ref, g_ref, ids_ref, w_ref, gate_ref, wu_hbm, wd_hbm,
+    x_hbm, g_hbm, ids_hbm, w_hbm, gate_hbm, wu_hbm, wd_hbm,
     ig_ref, gg_ref, ug_hbm, dg_hbm,
-    wu, wd, s_tok, s_route, w_slot, swap_out, swap_in, t4, slots, xd,
+    inp, ids_ref, w_ref, gate_ref,
+    wu, wd, s_tok, s_route, w_slot, t4, slots, xd,
     gate_out, gate_in, gd_out, gd_in, up_s, hid, upd, ps, qd, zs, zr, xs, tr, tk, fr, grads,
-    w_sem, swap_sem, a1_s, a1_r, gate_s, gate_r, xy_s, xy_r, za_s, za_r, zb_s, zb_r,
+    in_sem, w_sem, swap_sem, a1_s, a1_r, gate_s, gate_r, xy_s, xy_r, za_s, za_r, zb_s, zb_r,
     own_s, own_r, opp_s, opp_r, rd_s, rd_r, rza_s, rza_r, rzb_s, rzb_r, rx_s, rx_r,
     rg_s, rg_r, fin_s, fin_r, out_sem,
 ):
@@ -60,6 +64,15 @@
             src_ref=src, dst_ref=dst, send_sem=send, recv_sem=recv, device_id=ids, device_id_type=MESH
         )
 
+    loads = [
+        pltpu.make_async_copy(src, dst, in_sem.at[i])
+        for i, (src, dst) in enumerate(
+            ((ids_hbm, ids_ref), (w_hbm, w_ref), (x_hbm, inp.at[0]), (g_hbm, inp.at[1]), (gate_hbm, gate_ref))
+        )
+    ]
+    for load in loads:
+        load.start()
+
     bar = pltpu.get_barrier_semaphore()
 
     def greet(**ids):
@@ -74,7 +87,7 @@
 
     @pl.loop(1, NE)
     def _(k):
-        greet(expert=xor(me, k))
+        greet(expert=partner(me, k))
 
     def weight_copies():
         made = []
@@ -92,121 +105,142 @@
     for made in weight_copies():
         made.start()
 
+    loads[0].wait()
+    loads[1].wait()
     lane = lax.broadcasted_iota(jnp.int32, (TOK, TOK), 1)
     sub = lax.broadcasted_iota(jnp.int32, (TOK, TOK), 0)
+    earlier = (sub < lane).astype(BF16)
+    lane4 = lax.broadcasted_iota(jnp.int32, (TOK, 4 * TOK), 1)
+    sub4 = 4 * lax.broadcasted_iota(jnp.int32, (TOK, 4 * TOK), 0)
+    spread = ((lane4 >= sub4) & (lane4 < sub4 + 4)).astype(BF16)
     ids = ids_ref[...].astype(F32)
     wts = w_ref[...]
-    ids_pad = jnp.zeros((TOK, TOK), F32)
-    w_pad = jnp.zeros((TOK, TOK), F32)
-    for j in range(4):
-        ids_pad = jnp.where(lane == j, ids[:, j : j + 1], ids_pad)
-        w_pad = jnp.where(lane == j, wts[:, j : j + 1], w_pad)
-    ids_t = ids_pad.T[0:8]
-    w_t = w_pad.T[0:8]
-    earlier = (sub < lane).astype(BF16)
-    hits = []
-    experts = [xor(me, k).astype(F32) for k in range(NE)]
-    for k in range(NE):
-        hits.append([(ids_t[j : j + 1] == experts[k]).astype(F32) for j in range(4)])
+    experts = [partner(me, jnp.int32(k)).astype(F32) for k in range(NE)]
+    hits = [[(ids[j : j + 1] == experts[k]).astype(F32) for j in range(4)] for k in range(NE)]
     named = jnp.concatenate([h[0] + h[1] + h[2] + h[3] for h in hits], axis=0)
     rank = jnp.dot(named.astype(BF16), earlier, preferred_element_type=F32)
+    rank4 = jnp.dot(rank.astype(BF16), spread, preferred_element_type=F32)
+    ids_wide = jnp.dot(
+        jnp.concatenate([ids, ids], axis=0).astype(BF16), spread, preferred_element_type=F32
+    )
+    route = lax.rem(lax.broadcasted_iota(jnp.int32, (1, 4 * TOK), 1), 4)
+    ids4 = jnp.zeros((1, 4 * TOK), F32)
+    for j in range(4):
+        ids4 = jnp.where(route == j, ids_wide[j : j + 1], ids4)
     place = lax.broadcasted_iota(jnp.int32, (CAP, TOK), 0).astype(F32)
+    place4 = lax.broadcasted_iota(jnp.int32, (CAP, 4 * TOK), 0).astype(F32)
     for k in range(NE):
         here = jnp.where((rank[k : k + 1] == place) & (named[k : k + 1] > 0.5), 1.0, 0.0)
         rows = slice(k * CAP, (k + 1) * CAP)
         s_tok[rows] = here.astype(BF16)
         weight = jnp.zeros((1, TOK), F32)
         for j in range(4):
-            s_route[rows, j * TOK : (j + 1) * TOK] = (here * hits[k][j]).astype(BF16)
-            weight = weight + hits[k][j] * w_t[j : j + 1]
+            weight = weight + hits[k][j] * wts[j : j + 1]
         col = jnp.sum(here * weight, axis=1, keepdims=True)
         w_slot[rows] = jnp.where(c == 0, jnp.ones((CAP, TOK), F32), jnp.broadcast_to(col, (CAP, TOK)))
-
+        here4 = jnp.where((rank4[k : k + 1] == place4) & (ids4 == experts[k]), 1.0, 0.0)
+        s_route[rows] = here4.astype(BF16)
+
+    loads[2].wait()
+    loads[3].wait()
+
+    def half(i):
+        return pl.ds(pl.multiple_of(192 * i, 192), 192)
+
+    t4[mz, half(c)] = inp[c]
     pl.semaphore_wait(bar, 24)
 
-    xv = x_ref[...].astype(F32)
-    gv = g_ref[...].astype(F32)
-    is0 = c == 0
-    own_half = jnp.where(is0, xv, gv)
-    swap_out[...] = jnp.where(is0, gv, xv).astype(BF16)
-    swap = copy(swap_out, swap_in, swap_sem.at[0], swap_sem.at[1], dp=sib)
+    swap = copy(inp.at[sib], t4.at[mz, half(c)], swap_sem.at[0], swap_sem.at[1], dp=sib)
     swap.start()
-
-    def gate_copy(k):
-        return copy(gate_out.at[block(k)], gate_in.at[block(k)], gate_s.at[k], gate_r.at[k], expert=xor(me, k))
-
-    swap.wait_recv()
-    got = swap_in[...].astype(F32)
-    t4[mz] = jnp.concatenate(
-        [jnp.where(is0, own_half, got), jnp.where(is0, got, own_half)], axis=1
-    ).astype(BF16)
+    copy(inp.at[sib], t4.at[mz, half(sib)], swap_sem.at[0], swap_sem.at[1], dp=sib).wait_recv()
 
     def a1_copy(j):
         return copy(t4.at[mz], t4.at[mz], a1_s.at[j - 1], a1_r.at[j - 1], tensor=lax.rem(z + 2 * j, 8))
 
     for j in (2, 1, 3):
         a1_copy(j).start()
-
-    @pl.loop(0, GROUPS)
-    def _(g):
-        value = jnp.dot(s_route[group_rows(g)], gate_ref[...], preferred_element_type=F32)
-        gate_out[group_rows(g)] = value.astype(BF16)
-
-        @pl.when(g == 0)
-        def _():
-            gate_in[0:CAP] = value[0:CAP].astype(BF16)
-
-        for i in range(PER):
-            k = g * PER + i
-
-            @pl.when(k > 0)
-            def _():
-                gate_copy(k).start()
 
     def a1_arrival(j):
         src = lax.rem(mz + 4 - j, 4)
         return copy(t4.at[src], t4.at[src], a1_s.at[j - 1], a1_r.at[j - 1], tensor=lax.rem(z + 2 * j, 8))
 
+    def xy_copy(k, m):
+        at = 4 * k + m
+        return copy(
+            slots.at[m, block(k)], xd.at[c, p, m, block(k)], xy_s.at[at], xy_r.at[at], expert=partner(me, k)
+        )
+
+    def fill(g, m):
+        rows = group_rows(g)
+        value = lax.dot_general(s_tok[rows], t4[m], NT, preferred_element_type=F32)
+        scale = w_slot[rows]
+        value = (value * jnp.concatenate([scale] * (CH // TOK), axis=1)).astype(BF16)
+        slots[m, rows] = value
+
+        @pl.when(g == 0)
+        def _():
+            xd[c, p, m, 0:CAP] = value[0:CAP]
+
+    def gate_copy(k):
+        return copy(gate_out.at[block(k)], gate_in.at[block(k)], gate_s.at[k], gate_r.at[k], expert=partner(me, k))
+
+    @pl.loop(0, GROUPS)
+    def _(g):
+        fill(g, mz)
+        for i in range(PER):
+            k = g * PER + i
+
+            @pl.when(k > 0)
+            def _():
+                xy_copy(k, mz).start()
+
+    loads[4].wait()
+    gate_rows = gate_ref[...].reshape(4 * TOK, CH)
+    for g in range(GROUPS):
+        value = jnp.dot(s_route[g * GROUP : (g + 1) * GROUP], gate_rows, preferred_element_type=F32).astype(BF16)
+        gate_out[g * GROUP : (g + 1) * GROUP] = value
+        if g == 0:
+            gate_in[0:CAP] = value[0:CAP]
+        for i in range(PER):
+            k = g * PER + i
+            if k > 0:
+                gate_copy(jnp.int32(k)).start()
+
     for j in (1, 3, 2):
         a1_arrival(j).wait_recv()
 
-    def xy_copy(k):
-        return copy(slots.at[block(k)], xd.at[c, p, block(k)], xy_s.at[k], xy_r.at[k], expert=xor(me, k))
+    def others():
+        return [lax.rem(mz + j, 4) for j in (1, 2, 3)]
+
+    def send(k):
+        for m in others():
+            xy_copy(k, m).start()
 
     @pl.loop(0, GROUPS)
     def _(g):
-        rows = group_rows(g)
-        for m in range(4):
-            value = jnp.dot(s_tok[rows], t4[m], preferred_element_type=F32)
-            scale = w_slot[rows]
-            value = (value * jnp.concatenate([scale] * (CH // TOK), axis=1)).astype(BF16)
-            slots[rows, m * CH : (m + 1) * CH] = value
-
-            @pl.when(g == 0)
-            def _():
-                xd[c, p, 0:CAP, m * CH : (m + 1) * CH] = value[0:CAP]
-
+        for m in others():
+            fill(g, m)
         for i in range(PER):
             k = g * PER + i
 
-            @pl.when(k > 0)
-            def _():
-                xy_copy(k).start()
+            @pl.when((k > 0) & (k < WINDOW))
+            def _():
+                send(k)
 
     def za_copy(k, par):
-        at = xd.at[c, par, block(k), pl.ds(0, 768)]
+        at = xd.at[c, par, pl.ds(0, 2), block(k)]
         return copy(at, at, za_s.at[k], za_r.at[k], tensor=right)
 
     def zb_copy(k, par):
-        at = xd.at[c, par, block(k), pl.ds(768, 768)]
+        at = xd.at[c, par, pl.ds(2, 2), block(k)]
         return copy(at, at, zb_s.at[k], zb_r.at[k], tensor=left)
 
     def own_copy(k, arr):
-        at = xd.at[arr, p, block(k)]
+        at = xd.at[arr, p, :, block(k)]
         return copy(at, at, own_s.at[k], own_r.at[k], dp=sib)
 
     def opp_copy(k, arr):
-        at = xd.at[arr, 1 - p, block(k)]
+        at = xd.at[arr, 1 - p, :, block(k)]
         return copy(at, at, opp_s.at[k], opp_r.at[k], dp=sib)
 
     def rd_copy(g):
@@ -219,22 +253,26 @@
         return copy(zs.at[g, 1], zr.at[g, 1], rzb_s.at[g], rzb_r.at[g], tensor=left)
 
     def rx_copy(k):
-        return copy(xs.at[:, block(k)], tr.at[:, block(k)], rx_s.at[k], rx_r.at[k], expert=xor(me, k))
+        return copy(xs.at[:, block(k)], tr.at[:, block(k)], rx_s.at[k], rx_r.at[k], expert=partner(me, k))
 
     def rg_copy(k):
-        return copy(gd_out.at[block(k)], gd_in.at[block(k)], rg_s.at[k], rg_r.at[k], expert=xor(me, k))
+        return copy(gd_out.at[block(k)], gd_in.at[block(k)], rg_s.at[k], rg_r.at[k], expert=partner(me, k))
+
+    def product(a, weights, rows):
+        total = None
+        for par in range(2):
+            wide = jnp.concatenate([xd[a, par, m, rows] for m in range(4)], axis=1)
+            term = jnp.dot(wide, weights[par], preferred_element_type=F32)
+            total = term if total is None else total + term
+        return total
 
     def compute_up(g):
-        rows = group_rows(g)
-
         @pl.when(g == 0)
         def _():
             for made in weight_copies():
                 made.wait()
 
-        up_s[...] = jnp.dot(xd[0, 0, rows], wu[0], preferred_element_type=F32) + jnp.dot(
-            xd[0, 1, rows], wu[1], preferred_element_type=F32
-        )
+        up_s[...] = product(0, wu, group_rows(g))
 
     def compute_down(g):
         rows = group_rows(g)
@@ -245,9 +283,7 @@
             def _():
                 gate_copy(k).wait_recv()
 
-        dhid = jnp.dot(xd[1, 0, rows], wd[0], preferred_element_type=F32) + jnp.dot(
-            xd[1, 1, rows], wd[1], preferred_element_type=F32
-        )
+        dhid = product(1, wd, rows)
         up = up_s[...]
         gate = gate_in[rows].astype(F32)
         s = 1.0 / (1.0 + jnp.exp(-gate))
@@ -306,11 +342,10 @@
                 rx_copy(k).start()
 
     def grad(a, par, m):
-        left_side = xd[a, par, :, m * CH : (m + 1) * CH]
         right_side = (upd if a == 0 else hid)[...]
         q = 2 * m + par
         rows = slice(q * CH, (q + 1) * CH)
-        grads[a, rows] = lax.dot_general(left_side, right_side, TN, preferred_element_type=F32).astype(BF16)
+        grads[a, rows] = lax.dot_general(xd[a, par, m], right_side, TN, preferred_element_type=F32).astype(BF16)
         grad_copy(a, q).start()
 
     def grad_copy(a, q):
@@ -327,11 +362,16 @@
         def _():
             @pl.when(step > 0)
             def _():
-                xy_copy(step).wait_recv()
+                for m in range(4):
+                    xy_copy(step, m).wait_recv()
 
             za_copy(step, p).start()
             zb_copy(step, p).start()
             own_copy(step, c).start()
+
+            @pl.when(step + WINDOW < NE)
+            def _():
+                send(step + WINDOW)
 
         @pl.when((step >= LAG_Z) & (step < NE + LAG_Z))
         def _():
@@ -358,28 +398,28 @@
 
                 @pl.when(g > 0)
                 def _():
+                    return_z(g - 1)
+
+            @pl.when(phase == 1)
+            def _():
+                compute_down(g)
+
+            @pl.when(phase == 2)
+            def _():
+                compute_partial(g)
+
+                @pl.when(g > 0)
+                def _():
                     return_xy(g - 1)
-
-            @pl.when(phase == 1)
-            def _():
-                compute_down(g)
-
-            @pl.when(phase == 2)
-            def _():
-                compute_partial(g)
-
-            @pl.when(phase == 3)
-            def _():
-                return_z(g)
 
     last = GROUPS - 1
     for job in jobs[0:3]:
         grad(*job)
     return_z(last)
-    for job in jobs[3:7]:
+    for job in jobs[3:8]:
         grad(*job)
     return_xy(last)
-    for job in jobs[7:12]:
+    for job in jobs[8:14]:
         grad(*job)
 
     @pl.loop(1, NE)
@@ -398,9 +438,9 @@
         return (fin_dest(mm) == z) & (c == h)
 
     for mm in range(2):
-        total = lax.dot_general(s_tok[...], tr[mm], TN, preferred_element_type=F32)
+        total = lax.dot_general(s_tok[...], tr[mm], TN, preferred_element_type=F32).T
         for h in range(2):
-            value = total[:, h * 192 : (h + 1) * 192].astype(BF16)
+            value = total[h * 192 : (h + 1) * 192].astype(BF16)
             tk[mm, h] = value
 
             @pl.when(fin_local(mm, h))
@@ -411,14 +451,16 @@
             def _():
                 fin_copy(mm, h).start()
 
-    for job in jobs[12:16]:
+    for job in jobs[14:16]:
         grad(*job)
 
     @pl.loop(1, NE)
     def _(k):
         rg_copy(k).wait_recv()
 
-    gg_ref[...] = lax.dot_general(s_route[...], gd_in[...], TN, preferred_element_type=F32).astype(BF16)
+    gg_ref[...] = (
+        lax.dot_general(s_route[...], gd_in[...], TN, preferred_element_type=F32).astype(BF16).reshape(TOK, 4, CH)
+    )
 
     swap.wait_send()
     for j in range(1, 4):
@@ -434,7 +476,8 @@
         @pl.when(k > 0)
         def _():
             gate_copy(k).wait_send()
-            xy_copy(k).wait_send()
+            for m in range(4):
+                xy_copy(k, m).wait_send()
             rx_copy(k).wait_send()
             rg_copy(k).wait_send()
 
@@ -455,7 +498,7 @@
                 fr.at[src], fr.at[src], fin_s.at[0], fin_r.at[src], tensor=right
             ).wait_recv()
 
-    total = g_ref[...].astype(F32)
+    total = inp[1].astype(F32)
     for src in range(4):
         total = total + fr[src].astype(F32)
     ig_ref[...] = total.astype(BF16)
@@ -467,8 +510,27 @@
                 fin_copy(mm, h).wait_send()
 
 
+def finish(ig_in, gg_in, ug_in, dg_in, ig, gg, ug, dg, ig_v, gg_v, ug_v, dg_v, sem_in, sem_out):
+    inward, outward = [], []
+    for src, mid, dst, parts in (
+        (ug_in, ug_v, ug, 4), (dg_in, dg_v, dg, 4), (gg_in, gg_v, gg, 1), (ig_in, ig_v, ig, 1)
+    ):
+        size = src.shape[1] // parts
+        for part in range(parts):
+            at = (0, pl.ds(part * size, size)) if parts > 1 else slice(None)
+            n = len(inward)
+            inward.append(pltpu.make_async_copy(src.at[at], mid.at[at], sem_in.at[n]))
+            outward.append(pltpu.make_async_copy(mid.at[at], dst.at[at], sem_out.at[n]))
+    for made in inward:
+        made.start()
+    for arrived, made in zip(inward, outward):
+        arrived.wait()
+        made.start()
+    for made in outward:
+        made.wait()
+
+
 def local(moe_input, grad_out, expert_ids, route_weight, gate_pre, up_weight, down_weight):
-    gates = jnp.swapaxes(gate_pre, 0, 1).reshape(4 * TOK, CH)
     vmem = pl.BlockSpec(memory_space=pltpu.VMEM)
     anywhere = pl.BlockSpec(memory_space=pl.ANY)
     dma = pltpu.SemaphoreType.DMA
@@ -476,27 +538,29 @@
     def scratch(*shape, dtype=BF16):
         return pltpu.VMEM(shape, dtype)
 
-    input_grad, gate_rows, up_grad, down_grad = pl.pallas_call(
+    results = pl.pallas_call(
         kernel,
         out_shape=(
-            jax.ShapeDtypeStruct((TOK, 192), BF16),
-            jax.ShapeDtypeStruct((4 * TOK, CH), BF16),
+            jax.ShapeDtypeStruct((192, TOK), BF16),
+            jax.ShapeDtypeStruct((TOK, 4, CH), BF16),
             jax.ShapeDtypeStruct(up_weight.shape, BF16),
             jax.ShapeDtypeStruct(down_weight.shape, BF16),
         ),
-        in_specs=[vmem] * 5 + [anywhere] * 2,
+        in_specs=[anywhere] * 7,
         out_specs=(vmem, vmem, anywhere, anywhere),
         scratch_shapes=[
+            scratch(2, 192, TOK),
+            scratch(4, TOK, dtype=jnp.int32),
+            scratch(4, TOK, dtype=F32),
+            scratch(TOK, 4, CH),
             scratch(2, 4 * CH, CH),
             scratch(2, 4 * CH, CH),
             scratch(ROWS, TOK),
             scratch(ROWS, 4 * TOK),
             scratch(ROWS, TOK, dtype=F32),
-            scratch(TOK, 192),
-            scratch(TOK, 192),
-            scratch(4, TOK, CH),
-            scratch(ROWS, 4 * CH),
-            scratch(2, 2, ROWS, 4 * CH),
+            scratch(4, CH, TOK),
+            scratch(4, ROWS, CH),
+            scratch(2, 2, 4, ROWS, CH),
             scratch(ROWS, CH),
             scratch(ROWS, CH),
             scratch(ROWS, CH),
@@ -510,14 +574,15 @@
             scratch(GROUPS, 2, GROUP, CH),
             scratch(2, ROWS, CH),
             scratch(2, ROWS, CH),
-            scratch(2, 2, TOK, 192),
-            scratch(4, TOK, 192),
+            scratch(2, 2, 192, TOK),
+            scratch(4, 192, TOK),
             scratch(2, 8 * CH, CH),
+            dma((5,)),
             dma((16,)),
             dma((2,)),
             dma((3,)), dma((3,)),
             dma((NE,)), dma((NE,)),
-            dma((NE,)), dma((NE,)),
+            dma((4 * NE,)), dma((4 * NE,)),
             dma((NE,)), dma((NE,)),
             dma((NE,)), dma((NE,)),
             dma((NE,)), dma((NE,)),
@@ -534,9 +599,17 @@
             collective_id=0, has_side_effects=True, vmem_limit_bytes=60 * 1024 * 1024
         ),
         name="routed_backward",
-    )(moe_input, grad_out, expert_ids, route_weight, gates, up_weight, down_weight)
-    gate_grad = jnp.swapaxes(gate_rows.reshape(4, TOK, CH), 0, 1)
-    return input_grad, gate_grad, up_grad, down_grad
+    )(moe_input.T, grad_out.T, expert_ids.T, route_weight.T, gate_pre, up_weight, down_weight)
+    input_grad, gate_grad, up_grad, down_grad = pl.pallas_call(
+        finish,
+        out_shape=tuple(jax.ShapeDtypeStruct(r.shape, r.dtype) for r in results),
+        in_specs=[anywhere] * 4,
+        out_specs=(anywhere,) * 4,
+        scratch_shapes=[scratch(*r.shape) for r in results] + [dma((10,)), dma((10,))],
+        compiler_params=pltpu.CompilerParams(vmem_limit_bytes=60 * 1024 * 1024),
+        name="results",
+    )(*results)
+    return input_grad.T, gate_grad, up_grad, down_grad
 
 
 def solution(mesh):

time: 161 us -> 117 us (0.73)
  Pallas kernels: 144 us -> 117 us
  local copies, waits for them, and re-layouts: 16.1 us -> 0 us
    pallas_call x1 -> x2, Pallas kernels: 144 us -> 117 us  [the longest x1 112 us: local(): pl.pallas_call(kernel, out_shape=(jax.ShapeDtypeStruct((192, TOK), BF16),...]
    unnamed x9 -> x0, local copies, waits for them, and re-layouts: 12.3 us -> none
    reshape x1 -> x0, local copies, waits for them, and re-layouts: 2.05 us -> none  [local(): gate_grad = jnp.swapaxes(gate_rows.reshape(4, TOK, CH), 0, 1)]
    transpose x1 -> x0, local copies, waits for them, and re-layouts: 1.79 us -> none  [local(): gates = jnp.swapaxes(gate_pre, 0, 1).reshape(4 * TOK, CH)]
where the time goes in v2:
time: 117 us
  Pallas kernels  117 us (100%)
    pallas_call x1, Pallas kernels, local(): pl.pallas_call(kernel, out_shape=(jax.ShapeDtypeStruct((192, TOK), BF16),...  112 us
    pallas_call x1, Pallas kernels, local(): pl.pallas_call(finish, out_shape=tuple((jax.ShapeDtypeStruct(r.shape, r.d...  4.48 us

profile of v2, /device:TPU:1, one launch (start us, length us, event | category | flops | bytes accessed | tf_op | source)
XLA Modules:
  0.0 117.3 jit_solution(1301542921367955373)
XLA Ops:
  0.6 112.1 %routed_backward.1 = (bf16[192,128]{1,0:T(8,128)(2,1)}, bf16[128,4,384]{2,1,0:T(4,128)(2,1)}, bf16[1,3072,384]{2,1,0:T(8,128)(2,1)}, bf16[1,3072,384]{2,1,0:T(8,128)(2,1)}) custom-call(bf16[192,128]{1,0:T(8,128)(2,1)} %bitcast.5, bf16[192,128]{1,0:T(8,128)(2,1)} %bitcast.6, s32[4,128]{1,0:T(4,128)} %bitcast.7, f32[4,128]{1,0:T(4,128)} %bitcast.8, ...), custom_call_target="tpu_custom_call" | custom-call | tf_op jit(solution)/shard_map/routed_backward/pallas_call | solution.py:541
  112.8 4.5 %results.1 = (bf16[192,128]{1,0:T(8,128)(2,1)}, bf16[128,4,384]{2,1,0:T(4,128)(2,1)}, bf16[1,3072,384]{2,1,0:T(8,128)(2,1)}, bf16[1,3072,384]{2,1,0:T(8,128)(2,1)}) custom-call(bf16[192,128]{1,0:T(8,128)(2,1)} %get-tuple-element.12.ig_in, bf16[128,4,384]{2,1,0:T(4,128)(2,1)} %get-tuple-element.13.gg_in, bf16[1,3072,384]{2,1,0:T(8,128)(2,1)} %get-tuple-element.14.ug_in, ...), custom_call_target="tpu_custom_call" | custom-call | tf_op jit(solution)/shard_map/results/pallas_call | solution.py:603

commit v3 on v2

--- a/solution.py
+++ b/solution.py
@@ -15,7 +15,8 @@
 TOK = 128
 ROWS = NE * CAP
 CH = 384
-GROUP = 256
+GROUP = 128
+FILL = 256
 WINDOW = 8
 GROUPS = ROWS // GROUP
 PER = GROUP // CAP
@@ -44,9 +45,9 @@
     x_hbm, g_hbm, ids_hbm, w_hbm, gate_hbm, wu_hbm, wd_hbm,
     ig_ref, gg_ref, ug_hbm, dg_hbm,
     inp, ids_ref, w_ref, gate_ref,
-    wu, wd, s_tok, s_route, w_slot, t4, slots, xd,
+    wu, wd, s_tok, s_route, w_slot, t4, t4_t, slots, xd,
     gate_out, gate_in, gd_out, gd_in, up_s, hid, upd, ps, qd, zs, zr, xs, tr, tk, fr, grads,
-    in_sem, w_sem, swap_sem, a1_s, a1_r, gate_s, gate_r, xy_s, xy_r, za_s, za_r, zb_s, zb_r,
+    in_sem, w_sem, a1_s, a1_r, gate_s, gate_r, xy_s, xy_r, za_s, za_r, zb_s, zb_r,
     own_s, own_r, opp_s, opp_r, rd_s, rd_r, rza_s, rza_r, rzb_s, rzb_r, rx_s, rx_r,
     rg_s, rg_r, fin_s, fin_r, out_sem,
 ):
@@ -150,29 +151,32 @@
     t4[mz, half(c)] = inp[c]
     pl.semaphore_wait(bar, 24)
 
-    swap = copy(inp.at[sib], t4.at[mz, half(c)], swap_sem.at[0], swap_sem.at[1], dp=sib)
-    swap.start()
-    copy(inp.at[sib], t4.at[mz, half(sib)], swap_sem.at[0], swap_sem.at[1], dp=sib).wait_recv()
-
-    def a1_copy(j):
-        return copy(t4.at[mz], t4.at[mz], a1_s.at[j - 1], a1_r.at[j - 1], tensor=lax.rem(z + 2 * j, 8))
-
+    def token_copy(j, h):
+        return copy(
+            inp.at[h], t4.at[mz, half(c)], a1_s.at[2 * j + h], a1_r.at[2 * j + c], tensor=lax.rem(z + 2 * j, 8), dp=h
+        )
+
+    def token_arrival(j, h):
+        src = lax.rem(mz + 4 - j, 4)
+        return copy(
+            inp.at[h], t4.at[src, half(h)], a1_s.at[2 * j + h], a1_r.at[2 * j + h], tensor=right, dp=sib
+        )
+
+    token_copy(0, sib).start()
     for j in (2, 1, 3):
-        a1_copy(j).start()
-
-    def a1_arrival(j):
-        src = lax.rem(mz + 4 - j, 4)
-        return copy(t4.at[src], t4.at[src], a1_s.at[j - 1], a1_r.at[j - 1], tensor=lax.rem(z + 2 * j, 8))
-
-    def xy_copy(k, m):
+        token_copy(j, c).start()
+        token_copy(j, sib).start()
+    token_arrival(0, sib).wait_recv()
+
+    peer = lax.rem(me + 1, NE)
+
+    def xy_copy(k, m, to=peer):
         at = 4 * k + m
-        return copy(
-            slots.at[m, block(k)], xd.at[c, p, m, block(k)], xy_s.at[at], xy_r.at[at], expert=partner(me, k)
-        )
+        return copy(slots.at[m, block(k)], xd.at[c, p, m, block(k)], xy_s.at[at], xy_r.at[at], expert=to)
 
     def fill(g, m):
-        rows = group_rows(g)
-        value = lax.dot_general(s_tok[rows], t4[m], NT, preferred_element_type=F32)
+        rows = pl.ds(pl.multiple_of(g * FILL, FILL), FILL)
+        value = jnp.dot(s_tok[rows], t4_t[m], preferred_element_type=F32)
         scale = w_slot[rows]
         value = (value * jnp.concatenate([scale] * (CH // TOK), axis=1)).astype(BF16)
         slots[m, rows] = value
@@ -181,47 +185,57 @@
         def _():
             xd[c, p, m, 0:CAP] = value[0:CAP]
 
-    def gate_copy(k):
-        return copy(gate_out.at[block(k)], gate_in.at[block(k)], gate_s.at[k], gate_r.at[k], expert=partner(me, k))
-
-    @pl.loop(0, GROUPS)
+    def gate_copy(k, to=peer):
+        return copy(gate_out.at[block(k)], gate_in.at[block(k)], gate_s.at[k], gate_r.at[k], expert=to)
+
+    t4_t[mz] = t4[mz].T
+
+    @pl.loop(0, ROWS // FILL)
     def _(g):
         fill(g, mz)
-        for i in range(PER):
-            k = g * PER + i
+        for i in range(FILL // CAP):
+            k = g * (FILL // CAP) + i
 
             @pl.when(k > 0)
             def _():
-                xy_copy(k, mz).start()
+                xy_copy(k, mz, partner(me, k)).start()
 
     loads[4].wait()
     gate_rows = gate_ref[...].reshape(4 * TOK, CH)
-    for g in range(GROUPS):
-        value = jnp.dot(s_route[g * GROUP : (g + 1) * GROUP], gate_rows, preferred_element_type=F32).astype(BF16)
-        gate_out[g * GROUP : (g + 1) * GROUP] = value
+    for g in range(4):
+        value = jnp.dot(s_route[g * 256 : (g + 1) * 256], gate_rows, preferred_element_type=F32).astype(BF16)
+        gate_out[g * 256 : (g + 1) * 256] = value
         if g == 0:
             gate_in[0:CAP] = value[0:CAP]
-        for i in range(PER):
-            k = g * PER + i
-            if k > 0:
-                gate_copy(jnp.int32(k)).start()
+        if g == 1:
+            for k in range(1, 5):
+                gate_copy(jnp.int32(k), partner(me, jnp.int32(k))).start()
 
     for j in (1, 3, 2):
-        a1_arrival(j).wait_recv()
+        for h in range(2):
+            token_arrival(j, h).wait_recv()
+    for j in (1, 3, 2):
+        src = lax.rem(mz + 4 - j, 4)
+        t4_t[src] = t4[src].T
 
     def others():
         return [lax.rem(mz + j, 4) for j in (1, 2, 3)]
 
     def send(k):
+        to = partner(me, k)
         for m in others():
-            xy_copy(k, m).start()
-
-    @pl.loop(0, GROUPS)
+            xy_copy(k, m, to).start()
+
+        @pl.when(k > 4)
+        def _():
+            gate_copy(k, to).start()
+
+    @pl.loop(0, ROWS // FILL)
     def _(g):
         for m in others():
             fill(g, m)
-        for i in range(PER):
-            k = g * PER + i
+        for i in range(FILL // CAP):
+            k = g * (FILL // CAP) + i
 
             @pl.when((k > 0) & (k < WINDOW))
             def _():
@@ -252,11 +266,11 @@
     def rzb_copy(g):
         return copy(zs.at[g, 1], zr.at[g, 1], rzb_s.at[g], rzb_r.at[g], tensor=left)
 
-    def rx_copy(k):
-        return copy(xs.at[:, block(k)], tr.at[:, block(k)], rx_s.at[k], rx_r.at[k], expert=partner(me, k))
-
-    def rg_copy(k):
-        return copy(gd_out.at[block(k)], gd_in.at[block(k)], rg_s.at[k], rg_r.at[k], expert=partner(me, k))
+    def rx_copy(k, to=peer):
+        return copy(xs.at[:, block(k)], tr.at[:, block(k)], rx_s.at[k], rx_r.at[k], expert=to)
+
+    def rg_copy(k, to=peer):
+        return copy(gd_out.at[block(k)], gd_in.at[block(k)], rg_s.at[k], rg_r.at[k], expert=to)
 
     def product(a, weights, rows):
         total = None
@@ -302,7 +316,7 @@
 
             @pl.when(k > 0)
             def _():
-                rg_copy(k).start()
+                rg_copy(k, partner(me, k)).start()
 
     def compute_partial(g):
         value = upd[group_rows(g)]
@@ -339,7 +353,7 @@
 
             @pl.when(k > 0)
             def _():
-                rx_copy(k).start()
+                rx_copy(k, partner(me, k)).start()
 
     def grad(a, par, m):
         right_side = (upd if a == 0 else hid)[...]
@@ -353,10 +367,10 @@
         return pltpu.make_async_copy(grads.at[a, rows], (ug_hbm, dg_hbm)[a].at[0, rows], out_sem.at[a * 8 + q])
 
     jobs = [(a, par, m) for a in range(2) for m in range(4) for par in range(2)]
-    LAG_Z, LAG_S, LAG_C = 2, 3, 4
+    LAG_Z, LAG_S, LAG_C = 2, 3, 3
     FIRST = PER - 1 + LAG_C
 
-    @pl.loop(0, FIRST + 4 * (GROUPS - 1) + 3)
+    @pl.loop(0, FIRST + PER * GROUPS)
     def _(step):
         @pl.when(step < NE)
         def _():
@@ -389,12 +403,13 @@
         @pl.when(step >= FIRST)
         def _():
             turn = step - FIRST
-            g = lax.div(turn, 4)
-            phase = lax.rem(turn, 4)
+            g = lax.div(turn, PER)
+            phase = lax.rem(turn, PER)
 
             @pl.when(phase == 0)
             def _():
                 compute_up(g)
+                compute_down(g)
 
                 @pl.when(g > 0)
                 def _():
@@ -402,10 +417,6 @@
 
             @pl.when(phase == 1)
             def _():
-                compute_down(g)
-
-            @pl.when(phase == 2)
-            def _():
                 compute_partial(g)
 
                 @pl.when(g > 0)
@@ -413,13 +424,13 @@
                     return_xy(g - 1)
 
     last = GROUPS - 1
+    for job in jobs[0:0]:
+        grad(*job)
+    return_z(last)
     for job in jobs[0:3]:
         grad(*job)
-    return_z(last)
-    for job in jobs[3:8]:
-        grad(*job)
     return_xy(last)
-    for job in jobs[8:14]:
+    for job in jobs[3:12]:
         grad(*job)
 
     @pl.loop(1, NE)
@@ -451,7 +462,7 @@
             def _():
                 fin_copy(mm, h).start()
 
-    for job in jobs[14:16]:
+    for job in jobs[12:16]:
         grad(*job)
 
     @pl.loop(1, NE)
@@ -462,9 +473,10 @@
         lax.dot_general(s_route[...], gd_in[...], TN, preferred_element_type=F32).astype(BF16).reshape(TOK, 4, CH)
     )
 
-    swap.wait_send()
-    for j in range(1, 4):
-        a1_copy(j).wait_send()
+    for j in range(4):
+        token_copy(j, sib).wait_send()
+        if j > 0:
+            token_copy(j, c).wait_send()
 
     @pl.loop(0, NE)
     def _(k):
@@ -559,6 +571,7 @@
             scratch(ROWS, 4 * TOK),
             scratch(ROWS, TOK, dtype=F32),
             scratch(4, CH, TOK),
+            scratch(4, TOK, CH),
             scratch(4, ROWS, CH),
             scratch(2, 2, 4, ROWS, CH),
             scratch(ROWS, CH),
@@ -579,8 +592,7 @@
             scratch(2, 8 * CH, CH),
             dma((5,)),
             dma((16,)),
-            dma((2,)),
-            dma((3,)), dma((3,)),
+            dma((8,)), dma((8,)),
             dma((NE,)), dma((NE,)),
             dma((4 * NE,)), dma((4 * NE,)),
             dma((NE,)), dma((NE,)),

time: 117 us -> 115 us (0.983)
  Pallas kernels: 117 us -> 114 us
    pallas_call x1, Pallas kernels: 112 us -> 109 us  [local(): pl.pallas_call(kernel, out_shape=(jax.ShapeDtypeStruct((192, TOK), BF16),...]
where the time goes in v3:
time: 115 us; the launch traced here: 114 us
  Pallas kernels  114 us (99%)
    pallas_call x1, Pallas kernels, local(): pl.pallas_call(kernel, out_shape=(jax.ShapeDtypeStruct((192, TOK), BF16),...  109 us
    pallas_call x1, Pallas kernels, local(): pl.pallas_call(finish, out_shape=tuple((jax.ShapeDtypeStruct(r.shape, r.d...  4.48 us

profile of v3, /device:TPU:1, one launch (start us, length us, event | category | flops | bytes accessed | tf_op | source)
XLA Modules:
  0.0 114.4 jit_solution(2142499254958383270)
XLA Ops:
  0.6 109.2 %routed_backward.1 = (bf16[192,128]{1,0:T(8,128)(2,1)}, bf16[128,4,384]{2,1,0:T(4,128)(2,1)}, bf16[1,3072,384]{2,1,0:T(8,128)(2,1)}, bf16[1,3072,384]{2,1,0:T(8,128)(2,1)}) custom-call(bf16[192,128]{1,0:T(8,128)(2,1)} %bitcast.5, bf16[192,128]{1,0:T(8,128)(2,1)} %bitcast.6, s32[4,128]{1,0:T(4,128)} %bitcast.7, f32[4,128]{1,0:T(4,128)} %bitcast.8, ...), custom_call_target="tpu_custom_call" | custom-call | tf_op jit(solution)/shard_map/routed_backward/pallas_call | solution.py:553
  109.8 4.5 %results.1 = (bf16[192,128]{1,0:T(8,128)(2,1)}, bf16[128,4,384]{2,1,0:T(4,128)(2,1)}, bf16[1,3072,384]{2,1,0:T(8,128)(2,1)}, bf16[1,3072,384]{2,1,0:T(8,128)(2,1)}) custom-call(bf16[192,128]{1,0:T(8,128)(2,1)} %get-tuple-element.12.ig_in, bf16[128,4,384]{2,1,0:T(4,128)(2,1)} %get-tuple-element.13.gg_in, bf16[1,3072,384]{2,1,0:T(8,128)(2,1)} %get-tuple-element.14.ug_in, ...), custom_call_target="tpu_custom_call" | custom-call | tf_op jit(solution)/shard_map/results/pallas_call | solution.py:615

commit v4 on v3

--- a/solution.py
+++ b/solution.py
@@ -409,11 +409,12 @@
             @pl.when(phase == 0)
             def _():
                 compute_up(g)
-                compute_down(g)
 
                 @pl.when(g > 0)
                 def _():
                     return_z(g - 1)
+
+                compute_down(g)
 
             @pl.when(phase == 1)
             def _():

time: 115 us -> 113 us (0.983)
  Pallas kernels: 114 us -> 112 us
    pallas_call x1, Pallas kernels: 109 us -> 108 us  [local(): pl.pallas_call(kernel, out_shape=(jax.ShapeDtypeStruct((192, TOK), BF16),...]
where the time goes in v4:
time: 113 us
  Pallas kernels  112 us (99%)
    pallas_call x1, Pallas kernels, local(): pl.pallas_call(kernel, out_shape=(jax.ShapeDtypeStruct((192, TOK), BF16),...  108 us
    pallas_call x1, Pallas kernels, local(): pl.pallas_call(finish, out_shape=tuple((jax.ShapeDtypeStruct(r.shape, r.d...  4.48 us

profile of v4, /device:TPU:1, one launch (start us, length us, event | category | flops | bytes accessed | tf_op | source)
XLA Modules:
  0.0 113.1 jit_solution(9186107716960122686)
XLA Ops:
  0.6 107.8 %routed_backward.1 = (bf16[192,128]{1,0:T(8,128)(2,1)}, bf16[128,4,384]{2,1,0:T(4,128)(2,1)}, bf16[1,3072,384]{2,1,0:T(8,128)(2,1)}, bf16[1,3072,384]{2,1,0:T(8,128)(2,1)}) custom-call(bf16[192,128]{1,0:T(8,128)(2,1)} %bitcast.5, bf16[192,128]{1,0:T(8,128)(2,1)} %bitcast.6, s32[4,128]{1,0:T(4,128)} %bitcast.7, f32[4,128]{1,0:T(4,128)} %bitcast.8, ...), custom_call_target="tpu_custom_call" | custom-call | tf_op jit(solution)/shard_map/routed_backward/pallas_call | solution.py:554
  108.5 4.5 %results.1 = (bf16[192,128]{1,0:T(8,128)(2,1)}, bf16[128,4,384]{2,1,0:T(4,128)(2,1)}, bf16[1,3072,384]{2,1,0:T(8,128)(2,1)}, bf16[1,3072,384]{2,1,0:T(8,128)(2,1)}) custom-call(bf16[192,128]{1,0:T(8,128)(2,1)} %get-tuple-element.12.ig_in, bf16[128,4,384]{2,1,0:T(4,128)(2,1)} %get-tuple-element.13.gg_in, bf16[1,3072,384]{2,1,0:T(8,128)(2,1)} %get-tuple-element.14.ug_in, ...), custom_call_target="tpu_custom_call" | custom-call | tf_op jit(solution)/shard_map/results/pallas_call | solution.py:616
